TPU v7x, 32 devices: a whole 2x2x4 slice. The times are simulated.
32 devices in a mesh: row: 2 (over core), lat: 8 (over z, x), grp: 2 (over y).
Axes of the slice: x: 2, y: 2, z: 4, core: 2. Of those that a mesh axis runs over, the one named last changes fastest.
Arguments:
- stream_in: bfloat16 [192, 3584], P(('lat', 'grp'), 'row'), may hold values from -36 to 36, as said below
- pre_gain: float32 [3584], P('row'), may hold values from 0.25 to 1.75
- gate_weight: bfloat16 [3584, 14336], P('row', ('lat', 'grp')), may hold values from -0.09375 to 0.09375
- up_weight: bfloat16 [3584, 14336], P('row', ('lat', 'grp')), may hold values from -0.09375 to 0.09375
- down_weight: bfloat16 [14336, 3584], P(('lat', 'grp'), 'row'), may hold values from -0.046875 to 0.046875
- post_gain: float32 [3584], P('row'), may hold values from 0.25 to 1.75
- enc_weight: float32 [3584, 16384], P('row', ('lat', 'grp')), may hold values from -0.09375 to 0.09375
- enc_bias: float32 [16384], P(('lat', 'grp')), may hold values from -3 to 3
- dec_weight: float32 [16384, 3584], P(('lat', 'grp'), 'row'), may hold values from -0.046875 to 0.046875
- dec_bias: float32 [3584], P('row'), may hold values from -3 to 3
Outputs:
- stream_out: bfloat16 [192, 3584], P(('lat', 'grp'), 'row')
- grad_enc: float32 [3584, 16384], P('row', ('lat', 'grp'))
- grad_enc_bias: float32 [16384], P(('lat', 'grp'))
- grad_dec: float32 [16384, 3584], P(('lat', 'grp'), 'row')
- grad_dec_bias: float32 [3584], P('row')
Inputs may be any that keep to these rules, and one draw needn't show every extreme that they name: `stream_in`: Real-valued activations with scales that differ over rows and features.
All inputs are finite; a program needn't handle non-finite values.
Results may differ from a plain program's by a relative error of at most 0.013.
Values may be sent and summed in bfloat16 or wider, within the bound.
A program may use at most 128 MiB of HBM per device.

v0:
```python
import math
import jax
import jax.numpy as jnp
from jax import lax
from jax.sharding import PartitionSpec as P

D = 3584
epsilon = 1e-06
sparsity = 0.2
sharpness = 4.0


def smooth_relu(value):
    return jax.nn.softplus(sharpness * value) / sharpness


def activate(summed, hidden_width):
    return (
        jax.nn.gelu(summed[:, :hidden_width], approximate=True) * summed[:, hidden_width:]
    ).astype(jnp.bfloat16)


def body(
    stream_in,
    pre_gain,
    gate_weight,
    up_weight,
    down_weight,
    post_gain,
    enc_weight,
    enc_bias,
    dec_weight,
    dec_bias,
):
    highest = lax.Precision.HIGHEST
    stream = stream_in.astype(jnp.float32)
    hidden_width = gate_weight.shape[1]
    squares = lax.psum(jnp.sum(stream * stream, axis=1), "row")
    normed = (stream * lax.rsqrt(squares[:, None] / D + epsilon) * pre_gain).astype(jnp.bfloat16)
    joined = jnp.concatenate([gate_weight, up_weight], axis=1)
    partial_proj = jnp.dot(
        lax.all_gather(normed, ("lat", "grp"), axis=0, tiled=True),
        joined,
        preferred_element_type=jnp.float32,
    )
    shares = lax.psum_scatter(partial_proj, "row", scatter_dimension=0, tiled=True)
    hidden = lax.all_gather(activate(shares, hidden_width), "row", axis=0, tiled=True)
    output = lax.psum_scatter(
        jnp.dot(hidden, down_weight, preferred_element_type=jnp.float32),
        ("lat", "grp"),
        scatter_dimension=0,
        tiled=True,
    )
    out_squares = lax.psum(jnp.sum(output * output, axis=1), "row")
    stream_out = (
        stream + output * lax.rsqrt(out_squares[:, None] / D + epsilon) * post_gain
    ).astype(jnp.bfloat16)
    relayed = lax.all_gather(stream_out, ("lat", "grp"), axis=0, tiled=True)
    inputs = relayed.astype(jnp.float32)
    scale = 1.0 / math.sqrt(inputs.shape[0])
    encoded = jnp.dot(inputs, enc_weight, precision=highest, preferred_element_type=jnp.float32)
    preact = lax.psum(encoded, "row") + enc_bias
    latents = smooth_relu(preact)
    partial_rec = jnp.dot(
        latents, dec_weight, precision=highest, preferred_element_type=jnp.float32
    )
    recon = lax.psum(partial_rec, ("lat", "grp"))
    residual_grad = (recon + dec_bias - inputs) * scale
    grad_dec = jnp.dot(
        latents.T, residual_grad, precision=highest, preferred_element_type=jnp.float32
    )
    grad_dec_bias = jnp.sum(residual_grad, axis=0)
    back_term = jnp.dot(
        residual_grad, dec_weight.T, precision=highest, preferred_element_type=jnp.float32
    )
    latent_grad = (
        lax.psum(back_term.astype(jnp.bfloat16), "row").astype(jnp.float32) + sparsity * scale
    )
    preact_grad = latent_grad * jax.nn.sigmoid(sharpness * preact)
    grad_enc = jnp.dot(inputs.T, preact_grad, precision=highest, preferred_element_type=jnp.float32)
    grad_enc_bias = jnp.sum(preact_grad, axis=0)
    return (stream_out, grad_enc, grad_enc_bias, grad_dec, grad_dec_bias)


def solution(mesh):
    placed = (
        P(("lat", "grp"), "row"),
        P("row"),
        P("row", ("lat", "grp")),
        P("row", ("lat", "grp")),
        P(("lat", "grp"), "row"),
        P("row"),
        P("row", ("lat", "grp")),
        P(("lat", "grp")),
        P(("lat", "grp"), "row"),
        P("row"),
    )
    return jax.shard_map(
        body,
        mesh=mesh,
        in_specs=placed,
        out_specs=(
            P(("lat", "grp"), "row"),
            P("row", ("lat", "grp")),
            P(("lat", "grp")),
            P(("lat", "grp"), "row"),
            P("row"),
        ),
        check_vma=False,
    )
```

profile of v0, /device:TPU:0, one launch (start us, length us, event | category | flops | bytes accessed | tf_op | source)
XLA Modules:
  0.0 402.0 jit_solution(2031803251081122726)
XLA Ops:
  7.2 0.0 copy-start
  7.2 0.0 reduce-scatter.4.cloned.1.call-start
  7.2 1.1 fusion.20
  8.3 2.6 psum.35
  10.9 0.9 fusion.24
  11.8 50.0 %all-gather = bf16[16,12,1792]{2,1,0:T(8,128)(2,1)} all-gather(bf16[1,12,1792]{2,1,0:T(8,128)(2,1)S(1)} %fusion.24), channel_id=1, replica_groups=mesh['row'=2,'lat'=8,'grp'=2] {'lat','grp'}, dimensions={0}, use_global_device_ids=true | all-gather | bytes 731136 | tf_op jit(solution)/shard_map/all_gather | solution.py:42
  61.9 2.1 reshape.23
  63.9 5.6 %fusion.1 = f32[192,1792]{1,0:T(8,128)} fusion(bf16[192,1792]{1,0:T(8,128)(2,1)} %reshape.23, bf16[1792,896]{1,0:T(8,128)(2,1)} %param.13, bf16[1792,896]{1,0:T(8,128)(2,1)} %param.12), kind=kOutput, calls=%fused_computation | convolution fusion | flops 1245970432 | bytes 8486912 | tf_op jit(solution)/shard_map/dot_general | solution.py:41
  69.5 0.0 reduce-scatter.4.cloned.1.call-update
  69.6 0.0 all-reduce.6.cloned.1.call-start
  69.6 4.8 %reduce-scatter.4.cloned.1.call-done = f32[96,1792]{1,0:T(8,128)} async-done(((f32[192,1792]{1,0:T(8,128)}), f32[96,1792]{1,0:T(8,128)}) %reduce-scatter.4.cloned.1.call-update) | async-done | bytes 688144 | tf_op jit(solution)/shard_map/reduce_scatter | solution.py:46
  74.4 1.2 fusion.14
  75.6 2.1 all_gather.10
  77.7 0.0 copy-done
  77.7 0.0 copy-start.9
  77.7 2.0 fusion.36
  79.6 0.0 copy-start.4
  79.6 0.0 copy-start.8
  79.6 52.9 %fusion = f32[16,1792]{1,0:T(8,128)S(1)} fusion(f32[192,1792]{1,0:T(8,128)} %fusion.36), kind=kCustom, calls=%all-reduce-scatter | all-reduce-scatter fusion | flops 458753 | bytes 1491456
  132.6 1.3 collective-permute-start.2
  133.9 4.5 %collective-permute-start.1 = (f32[16,1792]{1,0:T(8,128)S(1)}, f32[16,1792]{1,0:T(8,128)}, u32[]{:S(2)}, u32[]{:S(2)}) collective-permute-start(f32[16,1792]{1,0:T(8,128)S(1)} %fusion), channel_id=1, source_target_pairs={{0,2},{1,3},{2,4},{3,5},{4,6},{5,7},{6,8},{7,9},{8,10},{9,11},{10,... | collective-permute-start | bytes 344072
  138.4 2.2 collective-permute-start
  140.5 0.7 slice.10
  141.2 2.4 collective-permute-start.3
  143.6 0.0 copy-done.9
  143.6 0.6 dynamic-slice.4
  144.8 0.8 collective-permute-done.3
  145.6 0.0 collective-permute-done.2
  145.6 0.0 collective-permute-done.1
  145.6 0.0 collective-permute-done
  145.6 8.0 %concatenate.4 = f32[76,1792]{1,0:T(8,128)} concatenate(f32[12,1792]{1,0:T(8,128)} %collective-permute-done.3, f32[16,1792]{1,0:T(8,128)S(1)} %collective-permute-done.2, f32[16,1792]{1,0:T(8,128)} %collective-permute-done.1, f32[16,1792]{1,0:T(8,128)} %collective-permute-done, f32[16,1792]{1,0:T(8,128)S(1)} %fusion), dimensions={0} | concatenate | bytes 1089536
  153.6 1.0 multiply_reduce_fusion
  154.6 2.5 psum.36
  157.1 0.0 copy-done.4
  157.1 0.0 copy-done.8
  157.1 1.0 fusion.23
  158.1 0.0 copy-start.5
  158.2 47.7 %all-gather.1 = bf16[16,12,1792]{2,1,0:T(8,128)(2,1)} all-gather(bf16[1,12,1792]{2,1,0:T(8,128)(2,1)S(1)} %bitcast.14), channel_id=1, replica_groups=mesh['row'=2,'lat'=8,'grp'=2] {'lat','grp'}, dimensions={0}, use_global_device_ids=true | all-gather | bytes 731136 | tf_op jit(solution)/shard_map/all_gather | solution.py:58
  205.8 2.1 reshape.25
  207.9 0.0 copy-start.6
  207.9 7.3 %fusion.37 = f32[192,1024]{1,0:T(8,128)} fusion(bf16[192,1792]{1,0:T(8,128)(2,1)} %reshape.25, f32[1792,1024]{1,0:T(8,128)} %param.16), kind=kOutput, calls=%fused_computation.46 | convolution fusion | flops 4227858432 | bytes 8814592 | tf_op jit(solution)/shard_map/dot_general | solution.py:61
  215.2 0.0 copy-done.5
  215.2 0.0 all-reduce.6.cloned.1.call-update
  215.3 0.0 copy-start.7
  215.3 0.2 all-reduce.8.cloned.1.call-start
  215.5 15.0 %all-reduce.6.cloned.1.call-done = f32[192,1024]{1,0:T(8,128)} async-done(((f32[192,1024]{1,0:T(8,128)}), f32[192,1024]{1,0:T(8,128)}) %all-reduce.6.cloned.1.call-update) | async-done | bytes 786448 | tf_op jit(solution)/shard_map/psum | solution.py:62
  230.5 0.0 copy-done.6
  230.5 9.9 %fusion.17 = f32[192,1792]{1,0:T(8,128)} fusion(f32[1024,1792]{1,0:T(8,128)} %param.18, f32[192,1024]{1,0:T(8,128)} %all-reduce.6.cloned.1.call-done, f32[1024]{0:T(1024)S(1)} %copy-done.6), kind=kOutput, calls=%fused_computation.21 | convolution fusion | flops 4229627904 | bytes 9506816 | tf_op jit(solution)/shard_map/dot_general | solution.py:64
  240.4 0.0 all-reduce.8.cloned.1.call-update
  240.4 0.3 all-reduce.10.cloned.1.call-start
  240.7 116.4 %all-reduce.8.cloned.1.call-done = f32[192,1792]{1,0:T(8,128)} async-done(((f32[192,1792]{1,0:T(8,128)}), f32[192,1792]{1,0:T(8,128)}) %all-reduce.8.cloned.1.call-update) | async-done | bytes 1376272 | tf_op jit(solution)/shard_map/psum | solution.py:67
  357.0 0.0 copy-done.7
  357.0 12.0 %convolution_convert_fusion = bf16[192,1024]{1,0:T(8,128)(2,1)} fusion(f32[1024,1792]{1,0:T(8,128)} %param.18, bf16[192,1792]{1,0:T(8,128)(2,1)} %reshape.25, f32[192,1792]{1,0:T(8,128)} %all-reduce.8.cloned.1.call-done, f32[1792]{0:T(1024)S(1)} %copy-done.7), kind=kOutput, calls=%fused_computation.6 | convolution fusion | flops 4229431296 | bytes 9804800 | tf_op jit(solution)/shard_map/dot_general | solution.py:73
  369.0 0.0 all-reduce.10.cloned.1.call-update
  369.0 0.0 copy-start.1
  369.0 0.0 copy-start.3
  369.0 2.5 fusion.19
  371.5 0.0 copy-done.1
  371.5 0.0 copy-done.3
  371.5 10.1 %fusion.15 = f32[1024,1792]{1,0:T(8,128)} fusion(f32[192,1024]{1,0:T(8,128)S(1)} %copy-done.3, f32[1024]{0:T(1024)S(1)} %copy-done.6, bf16[192,1792]{1,0:T(8,128)(2,1)S(1)} %copy-done.1, f32[192,1792]{1,0:T(8,128)} %all-reduce.8.cloned.1.call-done, f32[1792]{0:T(1024)S(1)} %copy-done.7), kind=kOutput, calls=%fused_computation.20 | convolution fusion | flops 4231004160 | bytes 10202112 | tf_op jit(solution)/shard_map/dot_general | solution.py:69
  381.6 5.0 %all-reduce.10.cloned.1.call-done = bf16[192,1024]{1,0:T(8,128)(2,1)} async-done(((bf16[192,1024]{1,0:T(8,128)(2,1)}), bf16[192,1024]{1,0:T(8,128)(2,1)}) %all-reduce.10.cloned.1.call-update) | async-done | bytes 393232 | tf_op jit(solution)/shard_map/psum | solution.py:77
  386.6 2.2 fusion.34
  388.8 0.0 copy-done.2
  388.8 6.7 %fusion.35 = f32[1792,1024]{1,0:T(8,128)} fusion(bf16[192,1792]{1,0:T(8,128)(2,1)S(1)} %copy-done.2, bf16[192,1024]{1,0:T(8,128)(2,1)} %all-reduce.10.cloned.1.call-done, f32[192,1024]{1,0:T(8,128)} %all-reduce.6.cloned.1.call-done, f32[1024]{0:T(1024)S(1)} %copy-done.6), kind=kOutput, calls=%fused_computation.44 | convolution fusion | flops 4229431296 | bytes 9211904 | tf_op jit(solution)/shard_map/dot_general | solution.py:80
  (3 shorter events, 0.0 us)
Async XLA Ops:
  7.2 70.5 %copy-start = (bf16[896,1792]{1,0:T(8,128)(2,1)S(1)}, bf16[896,1792]{1,0:T(8,128)(2,1)}, u32[]{:S(2)}) copy-start(bf16[896,1792]{1,0:T(8,128)(2,1)} %param.14) | copy-start | bytes 9633796
  7.2 67.2 %reduce-scatter.4.cloned.1.call-start = ((), (), s32[]{:S(2)}) async-start(), calls=%async_computation.1 | async-start | bytes 2064384 | tf_op jit(solution)/shard_map/reduce_scatter | solution.py:46
  69.6 160.9 %all-reduce.6.cloned.1.call-start = ((), (), s32[]{:S(2)}) async-start(), calls=%async_computation.2 | async-start | bytes 1572864 | tf_op jit(solution)/shard_map/psum | solution.py:62
  77.7 65.9 %copy-start.9 = (u32[32]{0:T(128)S(1)}, u32[32]{0:T(128)}, u32[]{:S(2)}) copy-start(u32[32]{0:T(128)} %constant.30) | copy-start | bytes 388
  79.6 77.5 %copy-start.4 = (bf16[12,1792]{1,0:T(8,128)(2,1)S(1)}, bf16[12,1792]{1,0:T(8,128)(2,1)}, u32[]{:S(2)}) copy-start(bf16[12,1792]{1,0:T(8,128)(2,1)} %param.10) | copy-start | bytes 129028
  79.6 77.5 %copy-start.8 = (f32[1792]{0:T(1024)S(1)}, f32[1792]{0:T(1024)}, u32[]{:S(2)}) copy-start(f32[1792]{0:T(1024)} %param.15) | copy-start | bytes 21508
  132.6 13.1 %collective-permute-start.2 = (f32[16,1792]{1,0:T(8,128)S(1)}, f32[16,1792]{1,0:T(8,128)S(1)}, u32[]{:S(2)}, u32[]{:S(2)}) collective-permute-start(f32[16,1792]{1,0:T(8,128)S(1)} %fusion), channel_id=1, source_target_pairs={{0,3},{1,4},{2,5},{3,6},{4,7},{5,8},{6,9},{7,10},{8,11},{9,12},{10... | collective-permute-start | bytes 344072
  133.9 11.8 %collective-permute-start.1 = (f32[16,1792]{1,0:T(8,128)S(1)}, f32[16,1792]{1,0:T(8,128)}, u32[]{:S(2)}, u32[]{:S(2)}) collective-permute-start(f32[16,1792]{1,0:T(8,128)S(1)} %fusion), channel_id=1, source_target_pairs={{0,2},{1,3},{2,4},{3,5},{4,6},{5,7},{6,8},{7,9},{8,10},{9,11},{10,... | collective-permute-start | bytes 344072
  138.4 7.3 %collective-permute-start = (f32[16,1792]{1,0:T(8,128)S(1)}, f32[16,1792]{1,0:T(8,128)}, u32[]{:S(2)}, u32[]{:S(2)}) collective-permute-start(f32[16,1792]{1,0:T(8,128)S(1)} %fusion), channel_id=1, source_target_pairs={{0,1},{1,2},{2,3},{3,4},{4,5},{5,6},{6,7},{7,8},{8,9},{9,10},{10,1... | collective-permute-start | bytes 344072
  141.2 4.4 %collective-permute-start.3 = (f32[12,1792]{1,0:T(8,128)}, f32[12,1792]{1,0:T(8,128)}, u32[]{:S(2)}, u32[]{:S(2)}) collective-permute-start(f32[12,1792]{1,0:T(8,128)} %slice.10), channel_id=1, source_target_pairs={{0,4},{1,5},{2,6},{3,7},{4,8},{5,9},{6,10},{7,11},{8,12},{9,13},{1... | collective-permute-start | bytes 258056
  158.1 57.1 %copy-start.5 = (bf16[12,1792]{1,0:T(8,128)(2,1)}, bf16[12,1792]{1,0:T(8,128)(2,1)S(1)}, u32[]{:S(2)}) copy-start(bf16[12,1792]{1,0:T(8,128)(2,1)S(1)} %fusion.23) | copy-start | bytes 129028
  207.9 22.6 %copy-start.6 = (f32[1024]{0:T(1024)S(1)}, f32[1024]{0:T(1024)}, u32[]{:S(2)}) copy-start(f32[1024]{0:T(1024)} %param.17) | copy-start | bytes 12292
  215.3 141.7 %copy-start.7 = (f32[1792]{0:T(1024)S(1)}, f32[1792]{0:T(1024)}, u32[]{:S(2)}) copy-start(f32[1792]{0:T(1024)} %param.19) | copy-start | bytes 21508
  215.3 141.7 %all-reduce.8.cloned.1.call-start = ((), (), s32[]{:S(2)}) async-start(), calls=%async_computation.3 | async-start | bytes 2752512 | tf_op jit(solution)/shard_map/psum | solution.py:67
  240.4 146.2 %all-reduce.10.cloned.1.call-start = ((), (), s32[]{:S(2)}) async-start(), calls=%async_computation.4 | async-start | bytes 786432 | tf_op jit(solution)/shard_map/psum | solution.py:77
  369.0 2.5 copy-start.1
  369.0 2.5 copy-start.3
  386.6 2.2 copy-start.2
Sparse Core Ops, SparseCore 0:
  69.7 4.6 reduce-scatter.3
  215.4 15.0 all-reduce.5
  240.5 116.4 all-reduce.7
  369.1 17.4 all-reduce.9
where the time goes:
time: 403 us; the launch traced here: 402 us
  blocking collectives  158 us (39%)
  waiting for transfers between devices  142 us (35%)
  matrix products  53.5 us (13%)
  between operations  14.5 us (4%)
  local copies, waits for them, and re-layouts  13.4 us (3%)
  starting transfers between devices  10.9 us (3%)
  other arithmetic  9.95 us (2%)
    psum x1, waiting for transfers between devices, body(): recon = lax.psum(partial_rec, ('lat', 'grp'))  116 us
    unnamed x1, blocking collectives  52.9 us
    all_gather x1, blocking collectives, body(): lax.all_gather(normed, ('lat', 'grp'), axis=0, tiled=True)  50 us
    all_gather x1, blocking collectives, body(): relayed = lax.all_gather(stream_out, ('lat', 'grp'), axis=0, tiled=True)  47.7 us
    psum x1, waiting for transfers between devices, body(): preact = lax.psum(encoded, 'row') + enc_bias  15 us
    unnamed x25, local copies, waits for them, and re-layouts  13.4 us
    dot_general x1, matrix products, body(): jnp.dot(residual_grad, dec_weight.T, precision=highest, preferred_element...  12 us
    unnamed x4, starting transfers between devices  10.4 us
  transfers between devices with their start and end apart: 8, of which 5 were waited for; matrix products, arithmetic and copies ran while one was open for 3% of the time, Pallas kernels for 0%

commit v1 on v0

--- a/solution.py
+++ b/solution.py
@@ -64,7 +64,7 @@
     partial_rec = jnp.dot(
         latents, dec_weight, precision=highest, preferred_element_type=jnp.float32
     )
-    recon = lax.psum(partial_rec, ("lat", "grp"))
+    recon = lax.psum(lax.psum(partial_rec, "grp"), "lat")
     residual_grad = (recon + dec_bias - inputs) * scale
     grad_dec = jnp.dot(
         latents.T, residual_grad, precision=highest, preferred_element_type=jnp.float32

time: 403 us -> 423 us (1.050)
  waiting for transfers between devices: 142 us -> 162 us
    psum x1 -> x2, waiting for transfers between devices: 116 us -> 136 us  [body(): recon = lax.psum(lax.psum(partial_rec, 'grp'), 'lat')]
  transfers between devices with their start and end apart: 8 -> 9, of which waited for: 5 -> 6; matrix products, arithmetic and copies ran while one was open for 3% -> 3% of each run, Pallas kernels for 0% -> 0%
where the time goes in v1:
time: 423 us; the launch traced here: 422 us
  waiting for transfers between devices  162 us (38%)
  blocking collectives  158 us (37%)
  matrix products  53.5 us (13%)
  between operations  14.5 us (3%)
  local copies, waits for them, and re-layouts  13.4 us (3%)
  starting transfers between devices  11 us (3%)
  other arithmetic  9.95 us (2%)
    psum x2, waiting for transfers between devices, body(): recon = lax.psum(lax.psum(partial_rec, 'grp'), 'lat')  136 us
    unnamed x1, blocking collectives  52.9 us
    all_gather x1, blocking collectives, body(): lax.all_gather(normed, ('lat', 'grp'), axis=0, tiled=True)  50 us
    all_gather x1, blocking collectives, body(): relayed = lax.all_gather(stream_out, ('lat', 'grp'), axis=0, tiled=True)  47.7 us
    psum x1, waiting for transfers between devices, body(): preact = lax.psum(encoded, 'row') + enc_bias  15 us
    unnamed x25, local copies, waits for them, and re-layouts  13.4 us
    dot_general x1, matrix products, body(): jnp.dot(residual_grad, dec_weight.T, precision=highest, preferred_element...  12 us
    unnamed x4, starting transfers between devices  10.4 us
  transfers between devices with their start and end apart: 9, of which 6 were waited for; matrix products, arithmetic and copies ran while one was open for 3% of the time, Pallas kernels for 0%

profile of v1, /device:TPU:0, one launch (start us, length us, event | category | flops | bytes accessed | tf_op | source)
XLA Modules:
  0.0 422.4 jit_solution(6897547855615704474)
XLA Ops:
  7.2 0.0 copy-start
  7.2 0.0 reduce-scatter.4.cloned.1.call-start
  7.2 1.1 fusion.20
  8.3 2.6 psum.42
  10.9 0.9 fusion.24
  11.8 50.0 %all-gather = bf16[16,12,1792]{2,1,0:T(8,128)(2,1)} all-gather(bf16[1,12,1792]{2,1,0:T(8,128)(2,1)S(1)} %fusion.24), channel_id=1, replica_groups=mesh['row'=2,'lat'=8,'grp'=2] {'lat','grp'}, dimensions={0}, use_global_device_ids=true | all-gather | bytes 731136 | tf_op jit(solution)/shard_map/all_gather | solution.py:42
  61.9 2.1 reshape.23
  63.9 5.6 %fusion.1 = f32[192,1792]{1,0:T(8,128)} fusion(bf16[192,1792]{1,0:T(8,128)(2,1)} %reshape.23, bf16[1792,896]{1,0:T(8,128)(2,1)} %param.13, bf16[1792,896]{1,0:T(8,128)(2,1)} %param.12), kind=kOutput, calls=%fused_computation | convolution fusion | flops 1245970432 | bytes 8486912 | tf_op jit(solution)/shard_map/dot_general | solution.py:41
  69.5 0.0 reduce-scatter.4.cloned.1.call-update
  69.6 0.0 all-reduce.7.cloned.1.call-start
  69.6 4.8 %reduce-scatter.4.cloned.1.call-done = f32[96,1792]{1,0:T(8,128)} async-done(((f32[192,1792]{1,0:T(8,128)}), f32[96,1792]{1,0:T(8,128)}) %reduce-scatter.4.cloned.1.call-update) | async-done | bytes 688144 | tf_op jit(solution)/shard_map/reduce_scatter | solution.py:46
  74.4 1.2 fusion.14
  75.6 2.1 all_gather.10
  77.7 0.0 copy-done
  77.7 0.0 copy-start.9
  77.7 2.0 fusion.36
  79.6 0.0 copy-start.4
  79.6 52.9 %fusion = f32[16,1792]{1,0:T(8,128)S(1)} fusion(f32[192,1792]{1,0:T(8,128)} %fusion.36), kind=kCustom, calls=%all-reduce-scatter | all-reduce-scatter fusion | flops 458753 | bytes 1491456
  132.6 1.3 collective-permute-start.2
  133.9 4.5 %collective-permute-start.1 = (f32[16,1792]{1,0:T(8,128)S(1)}, f32[16,1792]{1,0:T(8,128)}, u32[]{:S(2)}, u32[]{:S(2)}) collective-permute-start(f32[16,1792]{1,0:T(8,128)S(1)} %fusion), channel_id=1, source_target_pairs={{0,2},{1,3},{2,4},{3,5},{4,6},{5,7},{6,8},{7,9},{8,10},{9,11},{10,... | collective-permute-start | bytes 344072
  138.4 2.2 collective-permute-start
  140.5 0.7 slice.10
  141.2 2.4 collective-permute-start.3
  143.6 0.0 copy-done.9
  143.6 0.6 dynamic-slice.4
  144.8 0.8 collective-permute-done.3
  145.6 0.0 collective-permute-done.2
  145.6 0.0 collective-permute-done.1
  145.6 0.0 collective-permute-done
  145.6 8.0 %concatenate.4 = f32[76,1792]{1,0:T(8,128)} concatenate(f32[12,1792]{1,0:T(8,128)} %collective-permute-done.3, f32[16,1792]{1,0:T(8,128)S(1)} %collective-permute-done.2, f32[16,1792]{1,0:T(8,128)} %collective-permute-done.1, f32[16,1792]{1,0:T(8,128)} %collective-permute-done, f32[16,1792]{1,0:T(8,128)S(1)} %fusion), dimensions={0} | concatenate | bytes 1089536
  153.6 1.0 multiply_reduce_fusion
  154.6 2.5 psum.43
  157.1 0.0 copy-done.4
  157.1 0.0 copy-done.8
  157.1 1.0 fusion.23
  158.1 0.0 copy-start.5
  158.2 47.7 %all-gather.1 = bf16[16,12,1792]{2,1,0:T(8,128)(2,1)} all-gather(bf16[1,12,1792]{2,1,0:T(8,128)(2,1)S(1)} %bitcast.14), channel_id=1, replica_groups=mesh['row'=2,'lat'=8,'grp'=2] {'lat','grp'}, dimensions={0}, use_global_device_ids=true | all-gather | bytes 731136 | tf_op jit(solution)/shard_map/all_gather | solution.py:58
  205.8 2.1 reshape.25
  207.9 7.3 %fusion.37 = f32[192,1024]{1,0:T(8,128)} fusion(bf16[192,1792]{1,0:T(8,128)(2,1)} %reshape.25, f32[1792,1024]{1,0:T(8,128)} %param.16), kind=kOutput, calls=%fused_computation.46 | convolution fusion | flops 4227858432 | bytes 8814592 | tf_op jit(solution)/shard_map/dot_general | solution.py:61
  215.2 0.0 copy-done.5
  215.2 0.0 all-reduce.7.cloned.1.call-update
  215.3 0.2 all-reduce.9.cloned.1.call-start
  215.5 15.0 %all-reduce.7.cloned.1.call-done = f32[192,1024]{1,0:T(8,128)} async-done(((f32[192,1024]{1,0:T(8,128)}), f32[192,1024]{1,0:T(8,128)}) %all-reduce.7.cloned.1.call-update) | async-done | bytes 786448 | tf_op jit(solution)/shard_map/psum | solution.py:62
  230.5 0.0 copy-done.6
  230.5 9.9 %fusion.17 = f32[192,1792]{1,0:T(8,128)} fusion(f32[1024,1792]{1,0:T(8,128)} %param.18, f32[192,1024]{1,0:T(8,128)} %all-reduce.7.cloned.1.call-done, f32[1024]{0:T(1024)S(1)} %copy-done.6), kind=kOutput, calls=%fused_computation.21 | convolution fusion | flops 4229627904 | bytes 9506816 | tf_op jit(solution)/shard_map/dot_general | solution.py:64
  240.4 0.0 all-reduce.9.cloned.1.call-update
  240.4 0.0 all-reduce.11.cloned.1.call-start
  240.4 48.5 %all-reduce.9.cloned.1.call-done = f32[192,1792]{1,0:T(8,128)} async-done(((f32[192,1792]{1,0:T(8,128)}), f32[192,1792]{1,0:T(8,128)}) %all-reduce.9.cloned.1.call-update) | async-done | bytes 1376272 | tf_op jit(solution)/shard_map/psum | solution.py:67
  288.9 0.0 all-reduce.11.cloned.1.call-update
  288.9 0.3 all-reduce.13.cloned.1.call-start
  289.2 87.9 %all-reduce.11.cloned.1.call-done = f32[192,1792]{1,0:T(8,128)} async-done(((f32[192,1792]{1,0:T(8,128)}), f32[192,1792]{1,0:T(8,128)}) %all-reduce.11.cloned.1.call-update) | async-done | bytes 1376272 | tf_op jit(solution)/shard_map/psum | solution.py:67
  377.1 0.0 copy-done.7
  377.1 12.0 %convolution_convert_fusion = bf16[192,1024]{1,0:T(8,128)(2,1)} fusion(f32[1024,1792]{1,0:T(8,128)} %param.18, bf16[192,1792]{1,0:T(8,128)(2,1)} %reshape.25, f32[192,1792]{1,0:T(8,128)} %all-reduce.11.cloned.1.call-done, f32[1792]{0:T(1024)S(1)} %copy-done.7), kind=kOutput, calls=%fused_computation.6 | convolution fusion | flops 4229431296 | bytes 9804800 | tf_op jit(solution)/shard_map/dot_general | solution.py:73
  389.1 0.0 all-reduce.13.cloned.1.call-update
  389.1 0.0 copy-start.1
  389.2 0.0 copy-start.3
  389.2 2.5 fusion.19
  391.7 0.0 copy-done.1
  391.7 0.0 copy-done.3
  391.7 10.1 %fusion.15 = f32[1024,1792]{1,0:T(8,128)} fusion(f32[192,1024]{1,0:T(8,128)S(1)} %copy-done.3, f32[1024]{0:T(1024)S(1)} %copy-done.6, bf16[192,1792]{1,0:T(8,128)(2,1)S(1)} %copy-done.1, f32[192,1792]{1,0:T(8,128)} %all-reduce.11.cloned.1.call-done, f32[1792]{0:T(1024)S(1)} %copy-done.7), kind=kOutput, calls=%fused_computation.20 | convolution fusion | flops 4231004160 | bytes 10202112 | tf_op jit(solution)/shard_map/dot_general | solution.py:69
  401.8 5.2 %all-reduce.13.cloned.1.call-done = bf16[192,1024]{1,0:T(8,128)(2,1)} async-done(((bf16[192,1024]{1,0:T(8,128)(2,1)}), bf16[192,1024]{1,0:T(8,128)(2,1)}) %all-reduce.13.cloned.1.call-update) | async-done | bytes 393232 | tf_op jit(solution)/shard_map/psum | solution.py:77
  407.0 2.2 fusion.34
  409.2 0.0 copy-done.2
  409.2 6.7 %fusion.35 = f32[1792,1024]{1,0:T(8,128)} fusion(bf16[192,1792]{1,0:T(8,128)(2,1)S(1)} %copy-done.2, bf16[192,1024]{1,0:T(8,128)(2,1)} %all-reduce.13.cloned.1.call-done, f32[192,1024]{1,0:T(8,128)} %all-reduce.7.cloned.1.call-done, f32[1024]{0:T(1024)S(1)} %copy-done.6), kind=kOutput, calls=%fused_computation.44 | convolution fusion | flops 4229431296 | bytes 9211904 | tf_op jit(solution)/shard_map/dot_general | solution.py:80
  (6 shorter events, 0.0 us)
Async XLA Ops:
  7.2 70.5 %copy-start = (bf16[896,1792]{1,0:T(8,128)(2,1)S(1)}, bf16[896,1792]{1,0:T(8,128)(2,1)}, u32[]{:S(2)}) copy-start(bf16[896,1792]{1,0:T(8,128)(2,1)} %param.14) | copy-start | bytes 9633796
  7.2 67.2 %reduce-scatter.4.cloned.1.call-start = ((), (), s32[]{:S(2)}) async-start(), calls=%async_computation.1 | async-start | bytes 2064384 | tf_op jit(solution)/shard_map/reduce_scatter | solution.py:46
  69.6 160.9 %all-reduce.7.cloned.1.call-start = ((), (), s32[]{:S(2)}) async-start(), calls=%async_computation.2 | async-start | bytes 1572864 | tf_op jit(solution)/shard_map/psum | solution.py:62
  77.7 65.9 %copy-start.9 = (u32[32]{0:T(128)S(1)}, u32[32]{0:T(128)}, u32[]{:S(2)}) copy-start(u32[32]{0:T(128)} %constant.30) | copy-start | bytes 388
  79.6 77.5 %copy-start.4 = (bf16[12,1792]{1,0:T(8,128)(2,1)S(1)}, bf16[12,1792]{1,0:T(8,128)(2,1)}, u32[]{:S(2)}) copy-start(bf16[12,1792]{1,0:T(8,128)(2,1)} %param.10) | copy-start | bytes 129028
  79.6 77.5 %copy-start.8 = (f32[1792]{0:T(1024)S(1)}, f32[1792]{0:T(1024)}, u32[]{:S(2)}) copy-start(f32[1792]{0:T(1024)} %param.15) | copy-start | bytes 21508
  132.6 13.1 %collective-permute-start.2 = (f32[16,1792]{1,0:T(8,128)S(1)}, f32[16,1792]{1,0:T(8,128)S(1)}, u32[]{:S(2)}, u32[]{:S(2)}) collective-permute-start(f32[16,1792]{1,0:T(8,128)S(1)} %fusion), channel_id=1, source_target_pairs={{0,3},{1,4},{2,5},{3,6},{4,7},{5,8},{6,9},{7,10},{8,11},{9,12},{10... | collective-permute-start | bytes 344072
  133.9 11.8 %collective-permute-start.1 = (f32[16,1792]{1,0:T(8,128)S(1)}, f32[16,1792]{1,0:T(8,128)}, u32[]{:S(2)}, u32[]{:S(2)}) collective-permute-start(f32[16,1792]{1,0:T(8,128)S(1)} %fusion), channel_id=1, source_target_pairs={{0,2},{1,3},{2,4},{3,5},{4,6},{5,7},{6,8},{7,9},{8,10},{9,11},{10,... | collective-permute-start | bytes 344072
  138.4 7.3 %collective-permute-start = (f32[16,1792]{1,0:T(8,128)S(1)}, f32[16,1792]{1,0:T(8,128)}, u32[]{:S(2)}, u32[]{:S(2)}) collective-permute-start(f32[16,1792]{1,0:T(8,128)S(1)} %fusion), channel_id=1, source_target_pairs={{0,1},{1,2},{2,3},{3,4},{4,5},{5,6},{6,7},{7,8},{8,9},{9,10},{10,1... | collective-permute-start | bytes 344072
  141.2 4.4 %collective-permute-start.3 = (f32[12,1792]{1,0:T(8,128)}, f32[12,1792]{1,0:T(8,128)}, u32[]{:S(2)}, u32[]{:S(2)}) collective-permute-start(f32[12,1792]{1,0:T(8,128)} %slice.10), channel_id=1, source_target_pairs={{0,4},{1,5},{2,6},{3,7},{4,8},{5,9},{6,10},{7,11},{8,12},{9,13},{1... | collective-permute-start | bytes 258056
  158.1 57.1 %copy-start.5 = (bf16[12,1792]{1,0:T(8,128)(2,1)}, bf16[12,1792]{1,0:T(8,128)(2,1)S(1)}, u32[]{:S(2)}) copy-start(bf16[12,1792]{1,0:T(8,128)(2,1)S(1)} %fusion.23) | copy-start | bytes 129028
  207.9 22.6 %copy-start.6 = (f32[1024]{0:T(1024)S(1)}, f32[1024]{0:T(1024)}, u32[]{:S(2)}) copy-start(f32[1024]{0:T(1024)} %param.17) | copy-start | bytes 12292
  215.3 73.7 %all-reduce.9.cloned.1.call-start = ((), (), s32[]{:S(2)}) async-start(), calls=%async_computation.3 | async-start | bytes 2752512 | tf_op jit(solution)/shard_map/psum | solution.py:67
  240.4 136.8 %copy-start.7 = (f32[1792]{0:T(1024)S(1)}, f32[1792]{0:T(1024)}, u32[]{:S(2)}) copy-start(f32[1792]{0:T(1024)} %param.19) | copy-start | bytes 21508
  240.4 136.8 %all-reduce.11.cloned.1.call-start = ((), (), s32[]{:S(2)}) async-start(), calls=%async_computation.4 | async-start | bytes 2752512 | tf_op jit(solution)/shard_map/psum | solution.py:67
  288.9 118.1 %all-reduce.13.cloned.1.call-start = ((), (), s32[]{:S(2)}) async-start(), calls=%async_computation.5 | async-start | bytes 786432 | tf_op jit(solution)/shard_map/psum | solution.py:77
  389.1 2.5 copy-start.1
  389.2 2.5 copy-start.3
  407.0 2.2 copy-start.2
Sparse Core Ops, SparseCore 0:
  69.7 4.6 reduce-scatter.3
  215.4 15.0 all-reduce.6
  240.5 48.3 all-reduce.8
  292.7 84.3 all-reduce.10
  389.3 17.6 all-reduce.12
